TPU v7x, 32 devices: a whole 2x2x4 slice. The times are simulated.
32 devices in a mesh: tile: 16 (over z, y, core), dir: 2 (over x).
Axes of the slice: x: 2, y: 2, z: 4, core: 2. Of those that a mesh axis runs over, the one named last changes fastest.
Arguments:
- spectrum: float32 [36, 36, 4096], P('dir', None, 'tile'), may hold values from 0.1 to 1
- depths: float32 [4096], P('tile'), may hold values from 2 to 200
- refraction: float32 [2, 4096], P(None, 'tile'), may hold values from -0.22 to 0.22
- edge_geometry: float32 [2, 8, 4096], P(None, None, 'tile'), may hold values from -0.9 to 0.9
- neighbours: int32 [8, 4096], P(None, 'tile'), may hold values from 0 to 287, as said below
- send_rows: int32 [512], P('tile'), may hold values from 0 to 255
- coupling: float32 [36], replicated, may hold values from 0.05 to 0.5
- quad_table: int32 [4, 1296], replicated, may hold values from 0 to 1296, as said below
Outputs:
- spectrum_next: float32 [36, 36, 4096], P('dir', None, 'tile')
Inputs may be any that keep to these rules, and one draw needn't show every extreme that they name: `neighbours`: slots of a point beyond its live ones hold the point's own local index and zero edge geometry; index q < 256 is the tile's own point q, 256 + i the i-th point received from the tile below, 272 + i the i-th from the tile above; only points near a tile's edge link to received points. `send_rows`: each tile's block of 32 entries lists first the local points read by the tile below, then those read by the tile above. `quad_table`: 1296 marks a component outside the frequency range; for bin b = j * 36 + i, every component lies in a direction j ± 1 to 4 (mod 36) and a frequency i ± 2 or 3.
All inputs are finite; a program needn't handle non-finite values.
Results may differ from a plain program's by a relative error of at most 0.0003.
Values sent between devices are 32-bit elements; how exact they have to be, the bound alone decides.
A program may use at most 64 MiB of HBM per device.

v0:
```python
import functools
import math

import jax
import jax.numpy as jnp
from jax import lax
from jax.experimental import pallas as pl
from jax.experimental.pallas import tpu as pltpu
from jax.sharding import PartitionSpec as P

plus_factor = 1.0 / 1.25**4
minus_factor = 1.0 / 0.75**4
cross_factor = 1.0 / 0.9375**4
f32, bf16, i32 = jnp.float32, jnp.bfloat16, jnp.int32
REACH = 4
PITCH = 40
PITCH_K = 48
CHUNK = 2
CHUNKS = 4
GROUP = 3


def iota(shape, dim):
    return lax.broadcasted_iota(i32, shape, dim)


def split(x):
    hi = x.astype(bf16)
    lo = (x - hi.astype(f32)).astype(bf16)
    return hi, lo


def one_hot(mask):
    return jnp.where(mask, 1.0, 0.0)


def rows_from(local):
    return lax.reshape(local, (local.shape[0] * local.shape[1], local.shape[2]))


def kernel(
    dirs, freqs, points, halo, slots, tiles,
    spec, dep, refr, geo, nb, srow, coup, table, out,
    e32, ehi, elo, acc, sbuf, rbuf, hsend, hrecv, xcat, spat, wgt, krow, kcol, tab, tabt,
    misc, misci, speed_r, turn_r,
    send_sem, recv_sem, hsend_sem, hrecv_sem,
):
    d = lax.axis_index("dir")
    t = lax.axis_index("tile")
    ndir = 2 * dirs
    bins = ndir * freqs
    first = d * dirs
    own = 2 * REACH
    other = {"dir": 1 - d}

    barrier = pltpu.get_barrier_semaphore()
    pl.semaphore_signal(barrier, inc=1, device_id=other)

    @pl.when(t > 0)
    def _():
        pl.semaphore_signal(barrier, inc=1, device_id={"tile": t - 1})

    @pl.when(t < tiles - 1)
    def _():
        pl.semaphore_signal(barrier, inc=1, device_id={"tile": t + 1})

    def chunk_copy(k):
        return pltpu.make_async_remote_copy(
            src_ref=sbuf.at[k], dst_ref=rbuf.at[k],
            send_sem=send_sem.at[k], recv_sem=recv_sem.at[k],
            device_id=other,
        )

    def chunk_first(k):
        return CHUNK * k if k < CHUNKS else dirs - CHUNK * (k - CHUNKS + 1)

    def chunk_slot(k):
        return own + dirs + CHUNK * k if k < CHUNKS else own - CHUNK * (k - CHUNKS + 1)

    order = [k + half for k in range(CHUNKS) for half in (0, CHUNKS)]
    for k in order:
        for a in range(CHUNK):
            sbuf[k, a * freqs : (a + 1) * freqs, :] = spec[chunk_first(k) + a]
    pl.semaphore_wait(barrier, 1 + (t > 0).astype(i32) + (t < tiles - 1).astype(i32))
    for k in order:
        chunk_copy(k).start()

    zero_tail = jnp.zeros((PITCH_K - PITCH, points), f32)
    e32[...] = jnp.zeros(e32.shape, f32)
    acc[...] = jnp.zeros(acc.shape, f32)

    def keep_split(w):
        hi, lo = split(jnp.concatenate([e32[w], zero_tail], 0))
        ehi[w] = hi
        elo[w] = lo

    for j in range(dirs):
        e32[own + j, 0:freqs, :] = spec[j]
    for j in range(dirs):
        keep_split(own + j)
    own_rows = rows_from(e32[own : own + dirs])
    hi, lo = split(own_rows)
    xcat[:, 0:points] = hi
    xcat[:, points : 2 * points] = lo

    misci[...] = jnp.full(misci.shape, -1, i32)
    misci[0:1, 0 : 2 * halo] = srow[...]
    lane8 = iota((8, 128), 1)
    listed = misci[...]
    down = jnp.where(lane8 < halo, listed, 0)
    up = jnp.where(lane8 < halo, pltpu.roll(listed, 128 - halo, 1), 0)
    for shift in (halo, 2 * halo, 4 * halo):
        down = down + pltpu.roll(down, shift, 1)
        up = up + pltpu.roll(up, shift, 1)
    both = jnp.concatenate([down, up], 1)[0:1]
    sel = one_hot(both == iota((points, 256), 0)).astype(bf16)
    edge = jnp.dot(xcat[:, 0 : 2 * points], jnp.concatenate([sel, sel], 0), preferred_element_type=f32)
    rows_group = GROUP * PITCH
    groups = dirs // GROUP
    lane_group = (iota((rows_group, 256), 1) % 128) // halo
    packed = jnp.zeros((rows_group, 256), f32)
    for r in range(groups):
        packed = jnp.where(lane_group == r, edge[r * rows_group : (r + 1) * rows_group], packed)
    hsend[0] = packed[:, 0:128]
    hsend[1] = packed[:, 128:256]

    def halo_copy(slot, target):
        return pltpu.make_async_remote_copy(
            src_ref=hsend.at[1 - slot], dst_ref=hrecv.at[slot],
            send_sem=hsend_sem.at[slot], recv_sem=hrecv_sem.at[slot],
            device_id={"tile": target},
        )

    @pl.when(t > 0)
    def _():
        halo_copy(1, t - 1).start()

    @pl.when(t < tiles - 1)
    def _():
        halo_copy(0, t + 1).start()

    tab[...] = jnp.full(tab.shape, bins, i32)
    tab[0:4, 0:bins] = table[...]
    raw = tab[...]
    bin_dir = (iota(raw.shape, 1) * 1821) >> 16
    rel = raw - (bin_dir - REACH) * freqs
    rel = jnp.where(rel < 0, rel + bins, rel)
    rel = jnp.where(rel >= bins, rel - bins, rel)
    rel_dir = (rel * 1821) >> 16
    rel_freq = rel - rel_dir * freqs
    rel_slot = jnp.where(rel_dir > REACH, rel_dir - 1, rel_dir)
    missing = raw >= bins
    tab[...] = jnp.where(missing, -1, rel_slot * PITCH + rel_freq)
    in_cols = jnp.where(missing, -1, rel_slot * PITCH_K + rel_freq)
    for b in range(raw.shape[1] // 128):
        block = jnp.concatenate([in_cols[:, 128 * b : 128 * (b + 1)], jnp.zeros((120, 128), i32)], 0)
        tabt[128 * b : 128 * (b + 1), :] = block.T
    kcol[...] = jnp.full(kcol.shape, -1, i32)
    for j in range(ndir):
        start = j * freqs
        kcol[j, 0:freqs, :] = tabt[start : start + freqs, :]
        base = start // 128 * 128
        pair = tab[:, base : base + 256]
        here = pltpu.roll(pair, (256 - (start - base)) % 256, 1)[:, 0:128]
        there = pltpu.roll(here, PITCH, 1)
        rolled = pltpu.roll(there, 8 - 2, 0)
        krow[j] = jnp.where(
            lane8 < freqs, here,
            jnp.where((lane8 >= PITCH) & (lane8 < PITCH + freqs), rolled, -1),
        )
    misc[...] = jnp.zeros(misc.shape, f32)
    misc[0:1, 0:freqs] = coup[...]
    diagonal = iota((PITCH, 128), 0) == iota((PITCH, 128), 1)
    coupling = jnp.sum(jnp.where(diagonal, misc[0:1, :], 0.0), axis=1, keepdims=True)
    coupling = jnp.broadcast_to(coupling, (PITCH, points))

    def quadruplets(w):
        j = lax.rem(first - own + w + ndir, ndir)
        cols = kcol[j]
        lanes = iota((PITCH, 2 * REACH * PITCH_K), 1)
        pick = jnp.concatenate([one_hot(cols[:, c : c + 1] == lanes) for c in range(4)], 0).astype(bf16)
        window = jnp.concatenate(
            [
                rows_from(ref[pl.ds(at, REACH)])
                for ref in (ehi, elo)
                for at in (w - REACH, w + 1)
            ],
            0,
        )
        values = jnp.dot(jnp.concatenate([pick, pick], 1), window, preferred_element_type=f32)
        e = e32[w]
        deltas = []
        for c in range(2):
            plus = values[2 * c * PITCH : (2 * c + 1) * PITCH]
            minus = values[(2 * c + 1) * PITCH : (2 * c + 2) * PITCH]
            deltas.append(
                coupling
                * e
                * (e * (plus * plus_factor + minus * minus_factor) - 2.0 * cross_factor * plus * minus)
            )
        stacked = jnp.concatenate(deltas + [jnp.zeros((128 - 2 * PITCH, points), f32)], 0)
        hi, lo = split(stacked)
        rows = krow[j]
        down_rows = iota((2 * REACH * PITCH, 128), 0)
        place = (one_hot(rows[0:1] == down_rows) + one_hot(rows[1:2] == down_rows)).astype(bf16)
        gained = jnp.dot(
            jnp.concatenate([place, place], 1), jnp.concatenate([hi, lo], 0), preferred_element_type=f32
        )
        gained = gained.reshape(2 * REACH, PITCH, points)
        acc[pl.ds(w - REACH, REACH)] += gained[0:REACH]
        acc[pl.ds(w + 1, REACH)] += gained[REACH : 2 * REACH]
        acc[w] += -2.0 * (deltas[0] + deltas[1])

    def inner(w, carry):
        quadruplets(w)
        return carry

    lax.fori_loop(own + REACH, own + dirs - REACH, inner, 0)

    step = iota((PITCH, points), 0).astype(f32)
    ratio = jnp.exp(step * math.log(1.1))
    wavenum = (2.0 * math.pi * 0.0418 * ratio) ** 2 / 9.81
    shallow = jnp.tanh(wavenum * dep[...])
    speed_r[...] = jnp.sqrt(shallow) / ratio
    turn_r[...] = 1.0 - shallow

    def trig(f, j):
        at = [f(2.0 * math.pi * ((j + s * dirs) % ndir) / ndir) for s in range(2)]
        return jnp.where(d == 0, jnp.float32(at[0]), jnp.float32(at[1]))

    def bend(j):
        return trig(math.sin, j) * refr[0:1] - trig(math.cos, j) * refr[1:2]

    for j in range(dirs):
        flux = trig(math.cos, j) * geo[0] + trig(math.sin, j) * geo[1]
        wgt[j] = jnp.maximum(-flux, 0.0)

    @pl.when(t > 0)
    def _():
        halo_copy(0, t).wait_recv()

    @pl.when(t == 0)
    def _():
        hrecv[0] = jnp.zeros(hrecv.shape[1:], f32)

    @pl.when(t < tiles - 1)
    def _():
        halo_copy(1, t).wait_recv()

    @pl.when(t == tiles - 1)
    def _():
        hrecv[1] = jnp.zeros(hrecv.shape[1:], f32)

    arrived = jnp.concatenate([hrecv[0], hrecv[1]], 1)
    spread = jnp.concatenate([jnp.where(lane_group == r, arrived, 0.0) for r in range(groups)], 0)
    hi, lo = split(spread)
    xcat[:, 2 * points : 2 * points + 256] = hi
    xcat[:, 2 * points + 256 : 2 * points + 512] = lo

    entry = iota((256, points), 0)
    local_ids = iota((points, points), 0)
    halo_ids = points + jnp.where(entry >= 128, halo, 0) + entry % halo
    for s in range(slots):
        who = nb[s : s + 1, :]
        local = one_hot(who == local_ids).astype(bf16)
        edge = one_hot(who == halo_ids).astype(bf16)
        chosen = jnp.dot(
            xcat[...], jnp.concatenate([local, local, edge, edge], 0), preferred_element_type=f32
        ).reshape(dirs, PITCH, points)
        term = wgt[:, s : s + 1, :] * chosen
        if s == 0:
            spat[...] = term
        else:
            spat[...] += term

    for j in range(dirs):
        e = e32[own + j]
        total = jnp.sum(wgt[j], axis=0, keepdims=True)
        turned = -jnp.abs(bend(j)) * e
        if j > 0:
            turned = turned + jnp.maximum(bend(j - 1), 0.0) * e32[own + j - 1]
        if j < dirs - 1:
            turned = turned - jnp.minimum(bend(j + 1), 0.0) * e32[own + j + 1]
        acc[own + j] += e + speed_r[...] * (spat[j] - total * e) + turn_r[...] * turned

    for k in range(CHUNKS):
        for c in (k, CHUNKS + k):
            chunk_copy(c).wait_recv()
            for a in range(CHUNK):
                w = chunk_slot(c) + a
                e32[w, 0:freqs, :] = rbuf[c, a * freqs : (a + 1) * freqs, :]
                keep_split(w)
        if k == 0:
            acc[own] += turn_r[...] * (jnp.maximum(bend(-1), 0.0) * e32[own - 1])
            acc[own + dirs - 1] -= turn_r[...] * (jnp.minimum(bend(dirs), 0.0) * e32[own + dirs])

        def outer(a, carry):
            quadruplets(own + dirs - REACH + CHUNK * k + a)
            quadruplets(own + REACH - 1 - CHUNK * k - a)
            return carry

        lax.fori_loop(0, CHUNK, outer, 0)

    for j in range(dirs):
        out[j] = acc[own + j, 0:freqs, :]

    for k in order:
        chunk_copy(k).wait_send()

    @pl.when(t > 0)
    def _():
        halo_copy(1, t).wait_send()

    @pl.when(t < tiles - 1)
    def _():
        halo_copy(0, t).wait_send()


def body(tiles, spectrum, depths, refraction, edge_geometry, neighbours, send_rows, coupling, quad_table):
    dirs, freqs, points = spectrum.shape
    halo = send_rows.shape[0] // 2
    slots = neighbours.shape[0]
    ndir = 2 * dirs
    window = dirs + 4 * REACH
    lanes = (ndir * freqs + 127) // 128 * 128 + 128
    scratch = [
        pltpu.VMEM((window, PITCH, points), f32),
        pltpu.VMEM((window, PITCH_K, points), bf16),
        pltpu.VMEM((window, PITCH_K, points), bf16),
        pltpu.VMEM((window, PITCH, points), f32),
        pltpu.VMEM((2 * CHUNKS, CHUNK * freqs, points), f32),
        pltpu.VMEM((2 * CHUNKS, CHUNK * freqs, points), f32),
        pltpu.VMEM((2, GROUP * PITCH, 128), f32),
        pltpu.VMEM((2, GROUP * PITCH, 128), f32),
        pltpu.VMEM((dirs * PITCH, 2 * points + 512), bf16),
        pltpu.VMEM((dirs, PITCH, points), f32),
        pltpu.VMEM((dirs, slots, points), f32),
        pltpu.VMEM((ndir, 8, 128), i32),
        pltpu.VMEM((ndir, PITCH, 128), i32),
        pltpu.VMEM((8, lanes), i32),
        pltpu.VMEM((lanes, 128), i32),
        pltpu.VMEM((8, 128), f32),
        pltpu.VMEM((8, 128), i32),
        pltpu.VMEM((PITCH, points), f32),
        pltpu.VMEM((PITCH, points), f32),
        pltpu.SemaphoreType.DMA((2 * CHUNKS,)),
        pltpu.SemaphoreType.DMA((2 * CHUNKS,)),
        pltpu.SemaphoreType.DMA((2,)),
        pltpu.SemaphoreType.DMA((2,)),
    ]
    return pl.pallas_call(
        functools.partial(kernel, dirs, freqs, points, halo, slots, tiles),
        out_shape=jax.ShapeDtypeStruct(spectrum.shape, f32),
        in_specs=[pl.BlockSpec(memory_space=pltpu.VMEM)] * 8,
        out_specs=pl.BlockSpec(memory_space=pltpu.VMEM),
        scratch_shapes=scratch,
        compiler_params=pltpu.CompilerParams(
            collective_id=0, has_side_effects=True, vmem_limit_bytes=40 * 1024 * 1024
        ),
    )(
        spectrum,
        depths.reshape(1, points),
        refraction,
        edge_geometry,
        neighbours,
        send_rows.reshape(1, 2 * halo),
        coupling.reshape(1, freqs),
        quad_table,
    )


def solution(mesh):
    in_specs = (
        P("dir", None, "tile"),
        P("tile"),
        P(None, "tile"),
        P(None, None, "tile"),
        P(None, "tile"),
        P("tile"),
        P(),
        P(),
    )
    out_specs = P("dir", None, "tile")
    return jax.shard_map(
        functools.partial(body, mesh.shape["tile"]),
        mesh=mesh, in_specs=in_specs, out_specs=out_specs, check_vma=False,
    )
```

profile of v0, /device:TPU:0, one launch (start us, length us, event | category | flops | bytes accessed | tf_op | source)
XLA Modules:
  0.0 26.0 jit_solution(538287990786151198)
XLA Ops:
  0.0 0.0 copy-start.7
  0.0 0.0 copy-start.4
  0.0 0.0 copy-start.5
  0.0 0.0 copy-start.6
  0.0 0.6 %copy-done.7 = f32[36]{0:T(128)S(1)} copy-done((f32[36]{0:T(128)S(1)}, f32[36]{0:T(128)}, u32[]{:S(2)}) %copy-start.7) | copy-done | bytes 168
  0.7 0.0 copy-done.4
  0.7 0.0 copy-done.5
  0.7 0.0 copy-done.6
  0.7 0.0 copy-start
  0.7 1.1 %copy-done = f32[18,36,256]{2,1,0:T(8,128)S(1)} copy-done((f32[18,36,256]{2,1,0:T(8,128)S(1)}, f32[18,36,256]{2,1,0:T(8,128)}, u32[]{:S(2)}) %copy-start) | copy-done | bytes 663576
  1.8 0.0 copy-start.1
  1.8 0.7 %copy-done.1 = s32[4,1296]{1,0:T(4,128)S(1)} copy-done((s32[4,1296]{1,0:T(4,128)S(1)}, s32[4,1296]{1,0:T(4,128)}, u32[]{:S(2)}) %copy-start.1) | copy-done | bytes 20760
  2.6 0.0 copy-start.2
  2.6 0.7 %copy-done.2 = f32[2,8,256]{2,1,0:T(8,128)S(1)} copy-done((f32[2,8,256]{2,1,0:T(8,128)S(1)}, f32[2,8,256]{2,1,0:T(8,128)}, u32[]{:S(2)}) %copy-start.2) | copy-done | bytes 16408
  3.3 0.0 copy-start.3
  3.3 0.7 %copy-done.3 = s32[8,256]{1,0:T(8,128)S(1)} copy-done((s32[8,256]{1,0:T(8,128)S(1)}, s32[8,256]{1,0:T(8,128)}, u32[]{:S(2)}) %copy-start.3) | copy-done | bytes 8216
  4.0 21.1 %shard_map.82 = f32[18,36,256]{2,1,0:T(8,128)S(1)} custom-call(f32[18,36,256]{2,1,0:T(8,128)S(1)} %copy-done, f32[1,256]{1,0:T(1,128)S(1)} %bitcast.3, f32[2,256]{1,0:T(2,128)S(1)} %copy-done.4, f32[2,8,256]{2,1,0:T(8,128)S(1)} %copy-done.2, s32[8,256]{1,0:T(8,128)S(1)} %copy-done.3, s32[1,32]{1,0:T(1,128)S(1)} %bitcast.4, f32[1,36]{1,0:T(1,128)S(1)} %bitcast.5, ...), custom_call_target="tpu_custom_call" | custom-call | tf_op jit(solution)/shard_map/pallas_call | solution.py:351
  25.1 0.9 %copy.10 = f32[18,36,256]{2,1,0:T(8,128)} copy(f32[18,36,256]{2,1,0:T(8,128)S(1)} %shard_map.82) | data formatting | bytes 1327104
Async XLA Ops:
  0.0 0.7 %copy-start.7 = (f32[36]{0:T(128)S(1)}, f32[36]{0:T(128)}, u32[]{:S(2)}) copy-start(f32[36]{0:T(128)} %param.14) | copy-start | bytes 436
  0.0 0.7 %copy-start.4 = (f32[2,256]{1,0:T(2,128)S(1)}, f32[2,256]{1,0:T(2,128)}, u32[]{:S(2)}) copy-start(f32[2,256]{1,0:T(2,128)} %refr.1) | copy-start | bytes 6148
  0.0 0.7 %copy-start.5 = (f32[256]{0:T(256)S(1)}, f32[256]{0:T(256)}, u32[]{:S(2)}) copy-start(f32[256]{0:T(256)} %param.9) | copy-start | bytes 3076
  0.0 0.7 %copy-start.6 = (s32[32]{0:T(128)S(1)}, s32[32]{0:T(128)}, u32[]{:S(2)}) copy-start(s32[32]{0:T(128)} %param.13) | copy-start | bytes 388
  0.7 1.1 %copy-start = (f32[18,36,256]{2,1,0:T(8,128)S(1)}, f32[18,36,256]{2,1,0:T(8,128)}, u32[]{:S(2)}) copy-start(f32[18,36,256]{2,1,0:T(8,128)} %spec.1) | copy-start | bytes 1990660
  1.8 0.7 %copy-start.1 = (s32[4,1296]{1,0:T(4,128)S(1)}, s32[4,1296]{1,0:T(4,128)}, u32[]{:S(2)}) copy-start(s32[4,1296]{1,0:T(4,128)} %table.1) | copy-start | bytes 62212
  2.6 0.7 %copy-start.2 = (f32[2,8,256]{2,1,0:T(8,128)S(1)}, f32[2,8,256]{2,1,0:T(8,128)}, u32[]{:S(2)}) copy-start(f32[2,8,256]{2,1,0:T(8,128)} %geo.1) | copy-start | bytes 49156
  3.3 0.7 %copy-start.3 = (s32[8,256]{1,0:T(8,128)S(1)}, s32[8,256]{1,0:T(8,128)}, u32[]{:S(2)}) copy-start(s32[8,256]{1,0:T(8,128)} %nb.1) | copy-start | bytes 24580
where the time goes:
time: 26.3 us; the launch traced here: 26 us
  Pallas kernels  21.1 us (80%)
  local copies, waits for them, and re-layouts  4.84 us (18%)
    pallas_call x1, Pallas kernels, body(): pl.pallas_call(functools.partial(kernel, dirs, freqs, points, halo, slots...  21.1 us
    unnamed x17, local copies, waits for them, and re-layouts  4.84 us

commit v1 on v0

--- a/solution.py
+++ b/solution.py
@@ -17,6 +17,8 @@
 PITCH_K = 48
 CHUNK = 2
 CHUNKS = 4
+VMEM = 60 * 1024 * 1024
+BATCH = 5
 GROUP = 3
 
 
@@ -40,10 +42,10 @@
 
 def kernel(
     dirs, freqs, points, halo, slots, tiles,
-    spec, dep, refr, geo, nb, srow, coup, table, out,
-    e32, ehi, elo, acc, sbuf, rbuf, hsend, hrecv, xcat, spat, wgt, krow, kcol, tab, tabt,
+    spec, dep_h, refr_h, geo_h, nb_h, srow_h, coup_h, table_h, out,
+    e32, dep, refr, geo, nb, srow, coup, table, ehi, elo, acc, sbuf, rbuf, hsend, hrecv, xcat, spat, wgt, krow, kcol, tab, tabt,
     misc, misci, speed_r, turn_r,
-    send_sem, recv_sem, hsend_sem, hrecv_sem,
+    load_sem, send_sem, recv_sem, hsend_sem, hrecv_sem, out_sem,
 ):
     d = lax.axis_index("dir")
     t = lax.axis_index("tile")
@@ -78,31 +80,42 @@
         return own + dirs + CHUNK * k if k < CHUNKS else own - CHUNK * (k - CHUNKS + 1)
 
     order = [k + half for k in range(CHUNKS) for half in (0, CHUNKS)]
+    loads = [pltpu.make_async_copy(spec, e32.at[pl.ds(own, dirs)], load_sem.at[0])]
+    for i, (src, dst) in enumerate(
+        ((srow_h, srow), (table_h, table), (coup_h, coup), (nb_h, nb), (dep_h, dep), (refr_h, refr), (geo_h, geo))
+    ):
+        loads.append(pltpu.make_async_copy(src, dst, load_sem.at[i + 1]))
+    for load in loads:
+        load.start()
+    loads[0].wait()
     for k in order:
         for a in range(CHUNK):
-            sbuf[k, a * freqs : (a + 1) * freqs, :] = spec[chunk_first(k) + a]
+            sbuf[k, a * freqs : (a + 1) * freqs, :] = e32[own + chunk_first(k) + a]
     pl.semaphore_wait(barrier, 1 + (t > 0).astype(i32) + (t < tiles - 1).astype(i32))
     for k in order:
         chunk_copy(k).start()
 
     zero_tail = jnp.zeros((PITCH_K - PITCH, points), f32)
-    e32[...] = jnp.zeros(e32.shape, f32)
+    zero_rows = jnp.zeros((PITCH - freqs, points), f32)
     acc[...] = jnp.zeros(acc.shape, f32)
 
+    def full(w):
+        return jnp.concatenate([e32[w], zero_rows], 0)
+
     def keep_split(w):
-        hi, lo = split(jnp.concatenate([e32[w], zero_tail], 0))
+        hi, lo = split(jnp.concatenate([full(w), zero_tail], 0))
         ehi[w] = hi
         elo[w] = lo
 
     for j in range(dirs):
-        e32[own + j, 0:freqs, :] = spec[j]
-    for j in range(dirs):
         keep_split(own + j)
-    own_rows = rows_from(e32[own : own + dirs])
+    own_rows = jnp.concatenate([full(own + j) for j in range(dirs)], 0)
     hi, lo = split(own_rows)
     xcat[:, 0:points] = hi
     xcat[:, points : 2 * points] = lo
 
+    for load in loads[1:]:
+        load.wait()
     misci[...] = jnp.full(misci.shape, -1, i32)
     misci[0:1, 0 : 2 * halo] = srow[...]
     lane8 = iota((8, 128), 1)
@@ -174,21 +187,19 @@
     coupling = jnp.sum(jnp.where(diagonal, misc[0:1, :], 0.0), axis=1, keepdims=True)
     coupling = jnp.broadcast_to(coupling, (PITCH, points))
 
-    def quadruplets(w):
-        j = lax.rem(first - own + w + ndir, ndir)
+    pick_lanes = iota((PITCH, 2 * REACH * PITCH_K), 1)
+    place_rows = iota((2 * REACH * PITCH, 128), 0)
+
+    def gathered(w, j):
         cols = kcol[j]
-        lanes = iota((PITCH, 2 * REACH * PITCH_K), 1)
-        pick = jnp.concatenate([one_hot(cols[:, c : c + 1] == lanes) for c in range(4)], 0).astype(bf16)
+        pick = jnp.concatenate([one_hot(cols[:, c : c + 1] == pick_lanes) for c in range(4)], 0).astype(bf16)
         window = jnp.concatenate(
-            [
-                rows_from(ref[pl.ds(at, REACH)])
-                for ref in (ehi, elo)
-                for at in (w - REACH, w + 1)
-            ],
-            0,
-        )
-        values = jnp.dot(jnp.concatenate([pick, pick], 1), window, preferred_element_type=f32)
-        e = e32[w]
+            [rows_from(ref[pl.ds(at, REACH)]) for ref in (ehi, elo) for at in (w - REACH, w + 1)], 0
+        )
+        return jnp.dot(jnp.concatenate([pick, pick], 1), window, preferred_element_type=f32)
+
+    def exchanged(w, values):
+        e = full(w)
         deltas = []
         for c in range(2):
             plus = values[2 * c * PITCH : (2 * c + 1) * PITCH]
@@ -198,24 +209,33 @@
                 * e
                 * (e * (plus * plus_factor + minus * minus_factor) - 2.0 * cross_factor * plus * minus)
             )
+        return deltas
+
+    def scattered(w, j, deltas):
         stacked = jnp.concatenate(deltas + [jnp.zeros((128 - 2 * PITCH, points), f32)], 0)
         hi, lo = split(stacked)
         rows = krow[j]
-        down_rows = iota((2 * REACH * PITCH, 128), 0)
-        place = (one_hot(rows[0:1] == down_rows) + one_hot(rows[1:2] == down_rows)).astype(bf16)
+        place = (one_hot(rows[0:1] == place_rows) + one_hot(rows[1:2] == place_rows)).astype(bf16)
         gained = jnp.dot(
             jnp.concatenate([place, place], 1), jnp.concatenate([hi, lo], 0), preferred_element_type=f32
         )
-        gained = gained.reshape(2 * REACH, PITCH, points)
-        acc[pl.ds(w - REACH, REACH)] += gained[0:REACH]
-        acc[pl.ds(w + 1, REACH)] += gained[REACH : 2 * REACH]
-        acc[w] += -2.0 * (deltas[0] + deltas[1])
-
-    def inner(w, carry):
-        quadruplets(w)
+        return gained.reshape(2 * REACH, PITCH, points)
+
+    def quadruplets(slots_at):
+        js = [lax.rem(first - own + w + ndir, ndir) for w in slots_at]
+        values = [gathered(w, j) for w, j in zip(slots_at, js)]
+        deltas = [exchanged(w, v) for w, v in zip(slots_at, values)]
+        gains = [scattered(w, j, x) for w, j, x in zip(slots_at, js, deltas)]
+        for w, x, gained in zip(slots_at, deltas, gains):
+            acc[pl.ds(w - REACH, REACH)] += gained[0:REACH, 0:freqs]
+            acc[pl.ds(w + 1, REACH)] += gained[REACH : 2 * REACH, 0:freqs]
+            acc[w] += (-2.0 * (x[0] + x[1]))[0:freqs]
+
+    def inner(a, carry):
+        quadruplets([own + REACH + a * BATCH + b for b in range(BATCH)])
         return carry
 
-    lax.fori_loop(own + REACH, own + dirs - REACH, inner, 0)
+    lax.fori_loop(0, (dirs - 2 * REACH) // BATCH, inner, 0)
 
     step = iota((PITCH, points), 0).astype(f32)
     ratio = jnp.exp(step * math.log(1.1))
@@ -274,36 +294,44 @@
             spat[...] += term
 
     for j in range(dirs):
-        e = e32[own + j]
+        e = full(own + j)
         total = jnp.sum(wgt[j], axis=0, keepdims=True)
         turned = -jnp.abs(bend(j)) * e
         if j > 0:
-            turned = turned + jnp.maximum(bend(j - 1), 0.0) * e32[own + j - 1]
+            turned = turned + jnp.maximum(bend(j - 1), 0.0) * full(own + j - 1)
         if j < dirs - 1:
-            turned = turned - jnp.minimum(bend(j + 1), 0.0) * e32[own + j + 1]
-        acc[own + j] += e + speed_r[...] * (spat[j] - total * e) + turn_r[...] * turned
-
+            turned = turned - jnp.minimum(bend(j + 1), 0.0) * full(own + j + 1)
+        acc[own + j] += (e + speed_r[...] * (spat[j] - total * e) + turn_r[...] * turned)[0:freqs]
+
+    stores = []
     for k in range(CHUNKS):
         for c in (k, CHUNKS + k):
             chunk_copy(c).wait_recv()
             for a in range(CHUNK):
                 w = chunk_slot(c) + a
-                e32[w, 0:freqs, :] = rbuf[c, a * freqs : (a + 1) * freqs, :]
+                e32[w] = rbuf[c, a * freqs : (a + 1) * freqs, :]
                 keep_split(w)
         if k == 0:
-            acc[own] += turn_r[...] * (jnp.maximum(bend(-1), 0.0) * e32[own - 1])
-            acc[own + dirs - 1] -= turn_r[...] * (jnp.minimum(bend(dirs), 0.0) * e32[own + dirs])
-
-        def outer(a, carry):
-            quadruplets(own + dirs - REACH + CHUNK * k + a)
-            quadruplets(own + REACH - 1 - CHUNK * k - a)
-            return carry
-
-        lax.fori_loop(0, CHUNK, outer, 0)
-
-    for j in range(dirs):
-        out[j] = acc[own + j, 0:freqs, :]
-
+            acc[own] += turn_r[0:freqs] * (jnp.maximum(bend(-1), 0.0) * e32[own - 1])
+            acc[own + dirs - 1] -= turn_r[0:freqs] * (jnp.minimum(bend(dirs), 0.0) * e32[own + dirs])
+
+        quadruplets(
+            [own + dirs - REACH + CHUNK * k + a for a in range(CHUNK)]
+            + [own + REACH - 1 - CHUNK * k - a for a in range(CHUNK)]
+        )
+        low, high = 2 * REACH - 2 - CHUNK * k, dirs - 2 * REACH + 2 + CHUNK * k
+        parts = [(low, high)] if k == 0 else [(low, low + CHUNK), (high - CHUNK, high)]
+        for lo_dir, hi_dir in parts:
+            store = pltpu.make_async_copy(
+                acc.at[pl.ds(own + lo_dir, hi_dir - lo_dir)],
+                out.at[pl.ds(lo_dir, hi_dir - lo_dir)],
+                out_sem.at[len(stores)],
+            )
+            store.start()
+            stores.append(store)
+
+    for store in stores:
+        store.wait()
     for k in order:
         chunk_copy(k).wait_send()
 
@@ -324,10 +352,17 @@
     window = dirs + 4 * REACH
     lanes = (ndir * freqs + 127) // 128 * 128 + 128
     scratch = [
-        pltpu.VMEM((window, PITCH, points), f32),
+        pltpu.VMEM((window, freqs, points), f32),
+        pltpu.VMEM((1, points), f32),
+        pltpu.VMEM(refraction.shape, f32),
+        pltpu.VMEM(edge_geometry.shape, f32),
+        pltpu.VMEM(neighbours.shape, i32),
+        pltpu.VMEM((1, 2 * halo), i32),
+        pltpu.VMEM((1, freqs), f32),
+        pltpu.VMEM(quad_table.shape, i32),
         pltpu.VMEM((window, PITCH_K, points), bf16),
         pltpu.VMEM((window, PITCH_K, points), bf16),
-        pltpu.VMEM((window, PITCH, points), f32),
+        pltpu.VMEM((window, freqs, points), f32),
         pltpu.VMEM((2 * CHUNKS, CHUNK * freqs, points), f32),
         pltpu.VMEM((2 * CHUNKS, CHUNK * freqs, points), f32),
         pltpu.VMEM((2, GROUP * PITCH, 128), f32),
@@ -343,19 +378,21 @@
         pltpu.VMEM((8, 128), i32),
         pltpu.VMEM((PITCH, points), f32),
         pltpu.VMEM((PITCH, points), f32),
+        pltpu.SemaphoreType.DMA((8,)),
         pltpu.SemaphoreType.DMA((2 * CHUNKS,)),
         pltpu.SemaphoreType.DMA((2 * CHUNKS,)),
         pltpu.SemaphoreType.DMA((2,)),
         pltpu.SemaphoreType.DMA((2,)),
+        pltpu.SemaphoreType.DMA((2 * CHUNKS - 1,)),
     ]
     return pl.pallas_call(
         functools.partial(kernel, dirs, freqs, points, halo, slots, tiles),
         out_shape=jax.ShapeDtypeStruct(spectrum.shape, f32),
-        in_specs=[pl.BlockSpec(memory_space=pltpu.VMEM)] * 8,
-        out_specs=pl.BlockSpec(memory_space=pltpu.VMEM),
+        in_specs=[pl.BlockSpec(memory_space=pl.ANY)] * 8,
+        out_specs=pl.BlockSpec(memory_space=pl.ANY),
         scratch_shapes=scratch,
         compiler_params=pltpu.CompilerParams(
-            collective_id=0, has_side_effects=True, vmem_limit_bytes=40 * 1024 * 1024
+            collective_id=0, has_side_effects=True, vmem_limit_bytes=VMEM
         ),
     )(
         spectrum,

time: 26.3 us -> 22.1 us (0.84)
  local copies, waits for them, and re-layouts: 4.84 us -> 2.03 us
  Pallas kernels: 21.1 us -> 19.9 us
    unnamed x17 -> x1, local copies, waits for them, and re-layouts: 4.84 us -> 2.03 us
    pallas_call x1, Pallas kernels: 21.1 us -> 19.9 us  [body(): pl.pallas_call(functools.partial(kernel, dirs, freqs, points, halo, slots...]
where the time goes in v1:
time: 22.1 us; the launch traced here: 21.9 us
  Pallas kernels  19.9 us (90%)
  local copies, waits for them, and re-layouts  2.03 us (9%)
    pallas_call x1, Pallas kernels, body(): pl.pallas_call(functools.partial(kernel, dirs, freqs, points, halo, slots...  19.9 us
    unnamed x1, local copies, waits for them, and re-layouts  2.03 us

profile of v1, /device:TPU:0, one launch (start us, length us, event | category | flops | bytes accessed | tf_op | source)
XLA Modules:
  0.0 21.9 jit_solution(13342542581705365630)
XLA Ops:
  0.0 19.9 %shard_map.82 = f32[18,36,256]{2,1,0:T(8,128)} custom-call(f32[18,36,256]{2,1,0:T(8,128)} %spec.1, f32[1,256]{1,0:T(1,128)} %bitcast.3, f32[2,256]{1,0:T(2,128)} %refr_h.1, f32[2,8,256]{2,1,0:T(8,128)} %geo_h.1, s32[8,256]{1,0:T(8,128)} %nb_h.1, s32[1,32]{1,0:T(1,128)} %bitcast.4, f32[1,36]{1,0:T(1,128)} %bitcast.5, s32[4,1296]{1,0:T(4,128)} %table_h.1), custom_call_target="tpu_custom_call" | custom-call | tf_op jit(solution)/shard_map/pallas_call | solution.py:388
  19.9 2.0 %copy.10 = f32[18,36,256]{2,1,0:T(8,128)} copy(f32[18,36,256]{2,1,0:T(8,128)} %shard_map.82) | data formatting | bytes 1327104

commit v2 on v1

--- a/solution.py
+++ b/solution.py
@@ -17,7 +17,7 @@
 PITCH_K = 48
 CHUNK = 2
 CHUNKS = 4
-VMEM = 60 * 1024 * 1024
+VMEM = 61440 * 1024
 BATCH = 5
 GROUP = 3
 
@@ -45,7 +45,7 @@
     spec, dep_h, refr_h, geo_h, nb_h, srow_h, coup_h, table_h, out,
     e32, dep, refr, geo, nb, srow, coup, table, ehi, elo, acc, sbuf, rbuf, hsend, hrecv, xcat, spat, wgt, krow, kcol, tab, tabt,
     misc, misci, speed_r, turn_r,
-    load_sem, send_sem, recv_sem, hsend_sem, hrecv_sem, out_sem,
+    load_sem, send_sem, recv_sem, hsend_sem, hrecv_sem,
 ):
     d = lax.axis_index("dir")
     t = lax.axis_index("tile")
@@ -80,20 +80,27 @@
         return own + dirs + CHUNK * k if k < CHUNKS else own - CHUNK * (k - CHUNKS + 1)
 
     order = [k + half for k in range(CHUNKS) for half in (0, CHUNKS)]
-    loads = [pltpu.make_async_copy(spec, e32.at[pl.ds(own, dirs)], load_sem.at[0])]
+    def spec_load(at, count, sem):
+        return pltpu.make_async_copy(spec.at[pl.ds(at, count)], e32.at[pl.ds(own + at, count)], load_sem.at[sem])
+
+    middle = CHUNK * CHUNKS
+    spec_loads = [spec_load(chunk_first(k), CHUNK, i) for i, k in enumerate(order)]
+    spec_loads.append(spec_load(middle, dirs - 2 * middle, len(order)))
+    loads = []
     for i, (src, dst) in enumerate(
         ((srow_h, srow), (table_h, table), (coup_h, coup), (nb_h, nb), (dep_h, dep), (refr_h, refr), (geo_h, geo))
     ):
-        loads.append(pltpu.make_async_copy(src, dst, load_sem.at[i + 1]))
-    for load in loads:
+        loads.append(pltpu.make_async_copy(src, dst, load_sem.at[len(order) + 1 + i]))
+    for load in spec_loads + loads:
         load.start()
-    loads[0].wait()
-    for k in order:
+    for i, k in enumerate(order):
+        spec_loads[i].wait()
         for a in range(CHUNK):
             sbuf[k, a * freqs : (a + 1) * freqs, :] = e32[own + chunk_first(k) + a]
-    pl.semaphore_wait(barrier, 1 + (t > 0).astype(i32) + (t < tiles - 1).astype(i32))
-    for k in order:
+        if i == 0:
+            pl.semaphore_wait(barrier, 1 + (t > 0).astype(i32) + (t < tiles - 1).astype(i32))
         chunk_copy(k).start()
+    spec_loads[-1].wait()
 
     zero_tail = jnp.zeros((PITCH_K - PITCH, points), f32)
     zero_rows = jnp.zeros((PITCH - freqs, points), f32)
@@ -114,7 +121,7 @@
     xcat[:, 0:points] = hi
     xcat[:, points : 2 * points] = lo
 
-    for load in loads[1:]:
+    for load in loads:
         load.wait()
     misci[...] = jnp.full(misci.shape, -1, i32)
     misci[0:1, 0 : 2 * halo] = srow[...]
@@ -303,35 +310,27 @@
             turned = turned - jnp.minimum(bend(j + 1), 0.0) * full(own + j + 1)
         acc[own + j] += (e + speed_r[...] * (spat[j] - total * e) + turn_r[...] * turned)[0:freqs]
 
-    stores = []
-    for k in range(CHUNKS):
-        for c in (k, CHUNKS + k):
-            chunk_copy(c).wait_recv()
-            for a in range(CHUNK):
-                w = chunk_slot(c) + a
-                e32[w] = rbuf[c, a * freqs : (a + 1) * freqs, :]
-                keep_split(w)
-        if k == 0:
+    for i, c in enumerate(order):
+        chunk_copy(c).wait_recv()
+        for a in range(CHUNK):
+            w = chunk_slot(c) + a
+            e32[w] = rbuf[c, a * freqs : (a + 1) * freqs, :]
+            keep_split(w)
+        if c == 0:
+            acc[own + dirs - 1] -= turn_r[0:freqs] * (jnp.minimum(bend(dirs), 0.0) * e32[own + dirs])
+        if c == CHUNKS:
             acc[own] += turn_r[0:freqs] * (jnp.maximum(bend(-1), 0.0) * e32[own - 1])
-            acc[own + dirs - 1] -= turn_r[0:freqs] * (jnp.minimum(bend(dirs), 0.0) * e32[own + dirs])
-
-        quadruplets(
-            [own + dirs - REACH + CHUNK * k + a for a in range(CHUNK)]
-            + [own + REACH - 1 - CHUNK * k - a for a in range(CHUNK)]
-        )
-        low, high = 2 * REACH - 2 - CHUNK * k, dirs - 2 * REACH + 2 + CHUNK * k
-        parts = [(low, high)] if k == 0 else [(low, low + CHUNK), (high - CHUNK, high)]
-        for lo_dir, hi_dir in parts:
-            store = pltpu.make_async_copy(
-                acc.at[pl.ds(own + lo_dir, hi_dir - lo_dir)],
-                out.at[pl.ds(lo_dir, hi_dir - lo_dir)],
-                out_sem.at[len(stores)],
-            )
-            store.start()
-            stores.append(store)
-
-    for store in stores:
-        store.wait()
+        if c < CHUNKS:
+            quadruplets([chunk_slot(c) - REACH + a for a in range(CHUNK)])
+        else:
+            quadruplets([chunk_slot(c) + REACH + a for a in range(CHUNK)])
+        done = CHUNK * (c % CHUNKS + 1)
+        if i == 1:
+            out[2 * REACH - done : dirs - 2 * REACH + done] = acc[own + 2 * REACH - done : own + dirs - 2 * REACH + done]
+        elif i > 1:
+            at = dirs - 2 * REACH + done - CHUNK if c < CHUNKS else 2 * REACH - done
+            out[at : at + CHUNK] = acc[own + at : own + at + CHUNK]
+
     for k in order:
         chunk_copy(k).wait_send()
 
@@ -378,18 +377,17 @@
         pltpu.VMEM((8, 128), i32),
         pltpu.VMEM((PITCH, points), f32),
         pltpu.VMEM((PITCH, points), f32),
-        pltpu.SemaphoreType.DMA((8,)),
+        pltpu.SemaphoreType.DMA((2 * CHUNKS + 8,)),
         pltpu.SemaphoreType.DMA((2 * CHUNKS,)),
         pltpu.SemaphoreType.DMA((2 * CHUNKS,)),
         pltpu.SemaphoreType.DMA((2,)),
         pltpu.SemaphoreType.DMA((2,)),
-        pltpu.SemaphoreType.DMA((2 * CHUNKS - 1,)),
     ]
     return pl.pallas_call(
         functools.partial(kernel, dirs, freqs, points, halo, slots, tiles),
-        out_shape=jax.ShapeDtypeStruct(spectrum.shape, f32),
+        out_shape=pltpu.VMEM(spectrum.shape, f32),
         in_specs=[pl.BlockSpec(memory_space=pl.ANY)] * 8,
-        out_specs=pl.BlockSpec(memory_space=pl.ANY),
+        out_specs=pl.BlockSpec(memory_space=pltpu.VMEM),
         scratch_shapes=scratch,
         compiler_params=pltpu.CompilerParams(
             collective_id=0, has_side_effects=True, vmem_limit_bytes=VMEM

time: 22.1 us -> 19.9 us (0.900)
  local copies, waits for them, and re-layouts: 2.03 us -> 0.87 us
  Pallas kernels: 19.9 us -> 18.9 us
    unnamed x1, local copies, waits for them, and re-layouts: 2.03 us -> 0.87 us
    pallas_call x1, Pallas kernels: 19.9 us -> 18.9 us  [body(): pl.pallas_call(functools.partial(kernel, dirs, freqs, points, halo, slots...]
where the time goes in v2:
time: 19.9 us; the launch traced here: 19.8 us
  Pallas kernels  18.9 us (95%)
  local copies, waits for them, and re-layouts  0.87 us (4%)
    pallas_call x1, Pallas kernels, body(): pl.pallas_call(functools.partial(kernel, dirs, freqs, points, halo, slots...  18.9 us
    unnamed x1, local copies, waits for them, and re-layouts  0.87 us

profile of v2, /device:TPU:0, one launch (start us, length us, event | category | flops | bytes accessed | tf_op | source)
XLA Modules:
  0.0 19.8 jit_solution(2692159008802720829)
XLA Ops:
  0.0 18.9 %shard_map.82 = f32[18,36,256]{2,1,0:T(8,128)S(1)} custom-call(f32[18,36,256]{2,1,0:T(8,128)} %spec.1, f32[1,256]{1,0:T(1,128)} %bitcast.3, f32[2,256]{1,0:T(2,128)} %refr_h.1, f32[2,8,256]{2,1,0:T(8,128)} %geo_h.1, s32[8,256]{1,0:T(8,128)} %nb_h.1, s32[1,32]{1,0:T(1,128)} %bitcast.4, f32[1,36]{1,0:T(1,128)} %bitcast.5, s32[4,1296]{1,0:T(4,128)} %table_h.1), custom_call_target="tpu_custom_call" | custom-call | tf_op jit(solution)/shard_map/pallas_call | solution.py:386
  18.9 0.9 %copy.10 = f32[18,36,256]{2,1,0:T(8,128)} copy(f32[18,36,256]{2,1,0:T(8,128)S(1)} %shard_map.82) | data formatting | bytes 1327104
